TPU v7x, 768 devices: a whole 4x8x12 slice. The times are simulated.
768 devices in a mesh: dp: 64 (over x, y, core), text: 12 (over z).
Axes of the slice: x: 4, y: 8, z: 12, core: 2. Of those that a mesh axis runs over, the one named last changes fastest.
Arguments:
- regions: bfloat16 [128, 900, 256], P('dp', 'text'), may hold values from -6 to 6
- words: bfloat16 [128, 144, 256], P('dp', 'text'), may hold values from -6 to 6
- box_counts: int32 [128], P('dp'), may hold values from 100 to 900, as said below
- token_counts: int32 [128], P('dp'), may hold values from 72 to 144, as said below
- span_begin: int32 [128, 900], P('dp', 'text'), may hold values from 0 to 68
- span_length: int32 [128, 900], P('dp', 'text'), may hold values from 1 to 4
- bias_weight: float32 [256], replicated, may hold values from -0.375 to 0.375
- logit_bias: float32 [], replicated, may hold values from -1 to 0.5
- loss_scale: float32 [], replicated, may hold values from 512 to 2048
Outputs:
- region_grad: bfloat16 [128, 900, 256], P('dp', 'text')
- word_grad: bfloat16 [128, 144, 256], P('dp', 'text')
Inputs may be any that keep to these rules, and one draw needn't show every extreme that they name: `box_counts`: some image has exactly 900 boxes and some exactly 100. `token_counts`: some caption has exactly 144 tokens and some exactly 72.
All inputs are finite; a program needn't handle non-finite values.
Results may differ from a plain program's by a relative error of at most 0.0034.
Values may be sent and summed in bfloat16 or wider, within the bound.
A program may use at most 64 MiB of HBM per device.

v0:
```python
import math

import jax
import jax.numpy as jnp
from jax import lax
from jax.experimental import pallas as pl
from jax.experimental.pallas import tpu as pltpu
from jax.sharding import PartitionSpec as P

MESH = pl.DeviceIdType.MESH
NX, NY, NZ = 4, 8, 12
D = 256
HALF = 128
BOX = 75
BOXP = 80
RB = 2 * BOXP
TOK = 12
OWN = 2 * TOK
CB = 2 * OWN
GROUP = NZ * OWN
NEAR = 7
SHIFT = 3
SIDE = NY * RB
ROWS = 2 * SIDE
BF = jnp.bfloat16
F32 = jnp.float32
LOG2E = math.log2(math.e)
Z_ORDER = (1, 11, 2, 10, 3, 9, 4, 8, 5, 7, 6)
Z_NEAR = Z_ORDER[:6]
Z_FAR = Z_ORDER[6:]
Y_SIDES = ((0, 1, 7, 2), (6, 5, 3, 4))
PART = len(Y_SIDES[0]) * RB


def iota(shape, dim):
    return lax.broadcasted_iota(jnp.int32, shape, dim)


def negative_slope(score):
    grown = jnp.exp2(score)
    total = 1.0 + grown
    rest = 1.0 / total
    prob = grown * rest
    lost = jnp.log(total) + (grown - (total - 1.0))
    return prob * prob * (0.5 * prob + rest * lost)


def positive_slope(score):
    small = jnp.exp2(-jnp.abs(score))
    total = 1.0 + small
    part = 1.0 / total
    prob = jnp.where(score >= 0.0, part, small * part)
    rest = jnp.where(score >= 0.0, small * part, part)
    lost = jnp.log(total) + (small - (total - 1.0)) + jnp.maximum(-score, 0.0) * math.log(2.0)
    return (-1.0 / 6.0) * rest * rest * (2.0 * prob * lost + rest)


def kernel(
    regions, words, box_hbm, token_hbm, begin_hbm, length_hbm, bias_hbm, logit_hbm, scale_hbm,
    region_out, word_out,
    box, token, logit, scale, begin, length, bias,
    wide, rows, rows_t, limit, toks, w, wt, offset, g, wp, csum, rp,
    twin_out, twin_in, y_out, y_in, y_own, x_out, x_in, z_out, z_in,
    tally, tally_x, tally_z,
    l_sem, y_send, y_recv, z_send, z_recv, x_send, x_recv, c_send, c_recv, n_send, n_recv,
    ry_send, ry_recv, rx_send, rx_recv, rz_send, rz_recv,
):
    dp = lax.axis_index("dp")
    z = lax.axis_index("text")
    x, y, c = dp // (NY * 2), (dp // 2) % NY, dp % 2

    def at_x(k):
        return (((x + k) % NX) * NY + y) * 2 + c, z

    def at_y(k):
        return (x * NY + (y + k) % NY) * 2 + c, z

    def at_z(k):
        return dp, (z + k) % NZ

    twin = ((x * NY + y) * 2 + 1 - c, z)

    def send(src, dst, sends, recvs, k, dev):
        return pltpu.make_async_remote_copy(
            src_ref=src, dst_ref=dst, send_sem=sends.at[k], recv_sem=recvs.at[k], device_id=dev, device_id_type=MESH
        )

    barrier = pltpu.get_barrier_semaphore()
    peers = [at_z(k) for k in Z_ORDER] + [at_y(k) for k in (1, 7, 2, 6)] + [at_x(k) for k in (1, 3, 2)] + [twin]
    for dev in peers:
        pl.semaphore_signal(barrier, inc=1, device_id=dev, device_id_type=MESH)
    staged = (
        (box_hbm, box), (token_hbm, token), (begin_hbm, begin), (length_hbm, length), (bias_hbm, bias),
        (logit_hbm, logit), (scale_hbm, scale),
    )
    loads = [pltpu.make_async_copy(src, dst, l_sem.at[k]) for k, (src, dst) in enumerate(staged)]
    for load in loads:
        load.start()
    for load in loads:
        load.wait()

    tok = iota((TOK, D), 0)
    for cap in range(2):
        value = words[cap].astype(F32)
        wide[cap * TOK : (cap + 1) * TOK, :] = jnp.where(TOK * z + tok < token[cap], value, 0.0)
    mine = wide[0:OWN, :]
    toks[0, SHIFT] = jnp.concatenate([mine[:, 0:HALF], mine[:, HALF:D]], axis=0).astype(BF)

    count = jnp.zeros((1, 1), F32)
    for img in range(2):
        valid = BOX * z + iota((1, BOX), 1) < box[img]
        count = count + jnp.sum(jnp.where(valid, length[img : img + 1, :], 0).astype(F32), axis=1, keepdims=True)
    high = jnp.floor(count * (1.0 / 16.0))
    low = count - 16.0 * high
    lane, row = iota((BOXP, D), 1), iota((BOXP, D), 0)
    slot = jnp.where(lane < BOXP, lane, lane - BOXP)
    flag = (slot < BOX) & (lane < RB) & (BOX * z + slot < jnp.where(lane < BOXP, box[0], box[1]))
    for img in range(2):
        wide[img * BOXP + BOXP - 8 : (img + 1) * BOXP, :] = jnp.zeros((8, D), F32)
        wide[img * BOXP : img * BOXP + BOX, :] = regions[img].astype(F32)
        value = wide[img * BOXP : (img + 1) * BOXP, :]
        value = jnp.where((row < BOX) & (BOX * z + row < box[img]), value, 0.0)
        if img == 0:
            value = jnp.where((row == BOX) & flag, 1.0, value)
            value = jnp.where((row == BOX + 1) & (lane == 0), high, value)
            value = jnp.where((row == BOX + 1) & (lane == 1), low, value)
        rows[img * BOXP : (img + 1) * BOXP, :] = value.astype(BF)

    pl.semaphore_wait(barrier, len(peers))

    def where(r, other):
        side = 0 if r in Y_SIDES[0] else 1
        return (side * 2 + other) * PART + Y_SIDES[side].index(r) * RB

    def block(r, other=0):
        return rows.at[pl.ds(where(r, other), RB)]

    z_copies = {
        k: send(toks.at[0, SHIFT], toks.at[0, (SHIFT - k) % NZ], z_send, z_recv, k - 1, at_z(k)) for k in Z_ORDER
    }
    def half(r, k):
        return rows.at[pl.ds(where(r, 0) + k * BOXP, BOXP)]

    y_copies = {
        r: send(block(0), block(r), y_send, y_recv, k, at_y(NY - r)) for k, r in enumerate((7, 1, 6, 2))
    }
    y_copies[5] = send(block(6), block(5), y_send, y_recv, 4, at_y(1))
    y_copies[3] = send(block(2), block(3), y_send, y_recv, 5, at_y(7))
    y_copies[4] = send(half(6, 0), half(4, 0), y_send, y_recv, 6, at_y(2))
    y_copies[8] = send(half(2, 1), half(4, 1), y_send, y_recv, 7, at_y(6))
    twins = {r: send(block(r), block(r, 1), c_send, c_recv, r, twin) for r in range(NY)}
    near, far = pl.ds(0, NEAR), pl.ds(NEAR, NZ - NEAR)
    x_near = {k: send(toks.at[0, near], toks.at[NX - k, near], x_send, x_recv, k - 1, at_x(k)) for k in (2, 1, 3)}
    x_far = {k: send(toks.at[0, far], toks.at[NX - k, far], x_send, x_recv, 2 + k, at_x(k)) for k in (2, 1, 3)}
    for k in Z_ORDER:
        z_copies[k].start()
    for r in (7, 1, 6, 2):
        y_copies[r].start()
    twins[0].start()
    for k in Z_NEAR:
        z_copies[k].wait_recv()
    for copy in x_near.values():
        copy.start()

    def pass_on(r, onward=()):
        y_copies[r].wait_recv()
        for k in onward:
            y_copies[k].start()
        twins[r].start()

    pass_on(7)
    pass_on(1)
    pass_on(6, (5, 4))
    pass_on(2, (3, 8))
    for k in Z_FAR:
        z_copies[k].wait_recv()
    for copy in x_far.values():
        copy.start()

    def open_side(side):
        for r in Y_SIDES[side]:
            twins[r].wait_recv()
        total = jnp.zeros((1, 1), F32)
        span = slice(side * SIDE, (side + 1) * SIDE)
        rows_t[:, span] = jnp.transpose(rows[span, :])
        for r in range(side * NY, (side + 1) * NY):
            info = rows[r * RB + BOXP - 16 : r * RB + BOXP, :].astype(F32)
            flags = info[BOX - BOXP + 16 : BOX - BOXP + 17, 0:RB]
            limit[0:1, r * RB : (r + 1) * RB] = jnp.where(flags > 0.5, 100.0, -1000.0)
            count = info[BOX - BOXP + 17 : BOX - BOXP + 18, :]
            total = total + 16.0 * count[:, 0:1] + count[:, 1:2]
        return total

    bias_row = bias[...]
    logit_value = logit[0]

    def open_group(r):
        value = toks[r].astype(F32).reshape(NZ, 2, OWN, HALF)
        value = jnp.concatenate([value[:, 0].reshape(GROUP, HALF), value[:, 1].reshape(GROUP, HALF)], axis=1)
        w[r] = value.astype(BF)
        wt[r] = jnp.transpose(value).astype(BF)
        column = (jnp.sum(value * bias_row, axis=1, keepdims=True) + logit_value) * LOG2E
        offset[r] = jnp.broadcast_to(column, (GROUP, HALF))

    def line(ref, missing):
        pad = jnp.full((1, BOXP - BOX), missing, jnp.int32)
        rest = jnp.full((1, D - RB), missing, jnp.int32)
        return jnp.concatenate([ref[0:1, :], pad, ref[1:2, :], pad, rest], axis=1)

    def score_tile(r, side):
        span = slice(side * SIDE, (side + 1) * SIDE)
        raw = jnp.dot(w[r], rows_t[:, span], preferred_element_type=F32)
        score = jnp.minimum(raw * (LOG2E / 16.0) + offset[r][:, 0:1], limit[0:1, span])
        slope = negative_slope(score)
        if r == 0 and side == 0:
            start = line(begin, 1 << 20)
            stop = start + line(length, 0)
            index = iota((GROUP, D), 0)
            token_index = ((z + index // OWN + (NZ - SHIFT)) % NZ) * TOK + index % TOK
            image = (iota((GROUP, D), 1) >= BOXP).astype(jnp.int32)
            positive = (image == (index // TOK) % 2) & (token_index >= start) & (token_index < stop)
            positive = positive & (limit[0:1, 0:D] > 0.0)
            first = jnp.where(positive, positive_slope(score[:, 0:D]), slope[:, 0:D])
            slope = jnp.concatenate([first, slope[:, D:SIDE]], axis=1)
        total = slope[:, 0:HALF]
        for q in range(1, SIDE // HALF):
            total = total + slope[:, q * HALF : (q + 1) * HALF]
        g[side] = slope.astype(BF)
        return total

    def sum_tile(r, side, total, first_of_group, first_of_side):
        span = slice(side * SIDE, (side + 1) * SIDE)
        grads = jnp.dot(g[side], rows[span, :], preferred_element_type=F32)
        if first_of_group:
            wp[r] = grads
            csum[r] = total
        else:
            wp[r] = wp[r] + grads
            csum[r] = csum[r] + total
        part = jnp.dot(wt[r], g[side], preferred_element_type=F32)
        if first_of_side:
            rp[side] = part
        else:
            rp[side] = rp[side] + part

    def close_group(r):
        column = jnp.sum(csum[r], axis=1, keepdims=True)
        return wp[r] + column * (16.0 * bias_row)

    rx_copies = {k: send(x_out.at[k - 1], x_in.at[k - 1], rx_send, rx_recv, k - 1, at_x(k)) for k in (1, 2, 3)}
    ry_copies = {
        r: send(y_out.at[k], y_in.at[k], ry_send, ry_recv, k, at_y(to))
        for k, (r, to) in enumerate(((1, 1), (7, 7), (3, 1), (5, 7), (2, 2), (6, 6)))
    }
    upper, lower = pl.ds(0, BOXP), pl.ds(BOXP, BOXP)
    ry_copies[4] = send(y_out.at[6, upper], y_in.at[6, upper], ry_send, ry_recv, 6, at_y(2))
    ry_copies[8] = send(y_out.at[6, lower], y_in.at[6, lower], ry_send, ry_recv, 7, at_y(6))
    twin_copies = {
        side: send(twin_out.at[side], twin_in.at[side], c_send, c_recv, NY + side, twin) for side in range(2)
    }
    n_x = {k: send(tally.at[0], tally_x.at[k - 1], n_send, n_recv, k - 1, at_x(k)) for k in (1, 3, 2)}
    n_z = {k: send(tally.at[1], tally_z.at[k - 1], n_send, n_recv, 2 + k, at_z(k)) for k in Z_ORDER}

    def tile(r, side):
        total = score_tile(r, side)
        sum_tile(r, side, total, (r, side) in ((0, 0), (1, 0), (2, 0), (3, 1)), (r, side) in ((0, 0), (2, 1)))

    def words_of(r):
        x_near[NX - r].wait_recv()
        x_far[NX - r].wait_recv()
        open_group(r)

    def send_words(r):
        x_out[r - 1] = close_group(r).astype(BF)
        rx_copies[r].start()

    def other_core(side):
        twin_out[side] = jnp.transpose(rp[side][:, PART:SIDE]).astype(BF)
        twin_copies[side].start()

    def to_owners(side):
        twin_copies[side].wait_recv()
        both = jnp.transpose(rp[side][:, 0:PART]) + twin_in[side].astype(F32)
        kept = {0: 0, 2: 1, 6: 2}
        slots = {1: 0, 7: 1, 3: 2, 5: 3, 4: 6}
        for k, r in reversed(tuple(enumerate(Y_SIDES[side]))):
            part = both[k * RB : (k + 1) * RB, :]
            if r in kept:
                y_own[kept[r]] = part
            else:
                y_out[slots[r]] = part.astype(BF)
                ry_copies[r].start()
                if r == 4:
                    ry_copies[8].start()

    def pass_sums():
        for r, kept, near, far, part in ((2, 1, 3, 4, upper), (6, 2, 5, 8, lower)):
            slot, k = {2: 4, 6: 5}[r], {3: 2, 5: 3}[near]
            ry_copies[near].wait_recv()
            ry_copies[far].wait_recv()
            y_own[kept] = y_own[kept] + y_in[k].astype(F32)
            y_own[kept, part, :] = y_own[kept, part, :] + y_in[6, part, :].astype(F32)
            y_out[slot] = y_own[kept].astype(BF)
            ry_copies[r].start()

    open_group(0)
    counts = open_side(0)
    tile(0, 0)
    pass_on(5)
    pass_on(3)
    words_of(1)
    tile(1, 0)
    y_copies[8].wait_recv()
    pass_on(4)
    words_of(2)
    tile(2, 0)
    counts = counts + open_side(1)
    tally[0] = jnp.broadcast_to(counts, (8, HALF))
    for copy in n_x.values():
        copy.start()
    tile(2, 1)
    send_words(2)
    tile(0, 1)
    words_of(3)
    tile(1, 1)
    send_words(1)
    for copy in n_x.values():
        copy.wait_recv()
    tally[1] = tally[0] + tally_x[0] + tally_x[1] + tally_x[2]
    for copy in n_z.values():
        copy.start()
    tile(3, 1)
    other_core(1)
    tile(3, 0)
    other_core(0)
    send_words(3)
    to_owners(1)
    to_owners(0)

    sums = close_group(0)
    for k in (2, 1, 3):
        rx_copies[k].wait_recv()
        sums = sums + x_in[k - 1].astype(F32)
    sums = sums.reshape(NZ, OWN, D)
    halves = jnp.concatenate([sums[:, :, 0:HALF], sums[:, :, HALF:D]], axis=1)
    z_out[...] = halves.astype(BF)
    rz_copies = {
        k: send(z_out.at[(SHIFT + k) % NZ], z_in.at[k - 1], rz_send, rz_recv, k - 1, at_z(k)) for k in Z_ORDER
    }
    for k in reversed(Z_ORDER):
        rz_copies[k].start()
    chip = halves[SHIFT]
    pass_sums()

    positives = tally[1]
    for k in Z_ORDER:
        n_z[k].wait_recv()
        positives = positives + tally_z[k - 1]
    coef = (scale[0] * (1.5 / 16.0)) / positives[0:1, 0:1]

    for k in Z_ORDER:
        rz_copies[k].wait_recv()
        chip = chip + z_in[k - 1].astype(F32)
    value = jnp.concatenate([chip[0:OWN], chip[OWN:CB]], axis=1) * coef
    for cap in range(2):
        part = value[cap * TOK : (cap + 1) * TOK]
        word_out[cap] = jnp.where(TOK * z + tok < token[cap], part, 0.0).astype(BF)

    both = y_own[0]
    for k, r in ((0, 1), (1, 7), (4, 2), (5, 6)):
        ry_copies[r].wait_recv()
        both = both + y_in[k].astype(F32)
    for img in range(2):
        part = both[img * BOXP : (img + 1) * BOXP] * coef
        part = jnp.where(BOX * z + row < box[img], part, 0.0)
        region_out[img] = part[0:BOX].astype(BF)

    for copies in (z_copies, y_copies, twins, x_near, x_far, rx_copies, n_x, n_z, ry_copies, rz_copies, twin_copies):
        for copy in copies.values():
            copy.wait_send()


def on_device(
    regions,
    words,
    box_counts,
    token_counts,
    span_begin,
    span_length,
    bias_weight,
    logit_bias,
    loss_scale,
):
    vmem, in_hbm = pl.BlockSpec(memory_space=pltpu.VMEM), pl.BlockSpec(memory_space=pltpu.HBM)
    smem = pltpu.SMEM
    hold = pltpu.VMEM

    def sems(n):
        return [pltpu.SemaphoreType.DMA((n,))] * 2

    return pl.pallas_call(
        kernel,
        out_shape=(
            jax.ShapeDtypeStruct((2, BOX, D), BF),
            jax.ShapeDtypeStruct((2, TOK, D), BF),
        ),
        in_specs=[vmem] * 2 + [in_hbm] * 7,
        out_specs=(vmem, vmem),
        scratch_shapes=[
            smem((2,), jnp.int32),
            smem((2,), jnp.int32),
            smem((1,), F32),
            smem((1,), F32),
            hold((2, BOX), jnp.int32),
            hold((2, BOX), jnp.int32),
            hold((1, D), F32),
            hold((RB, D), F32),
            hold((ROWS, D), BF),
            hold((D, ROWS), BF),
            hold((8, ROWS), F32),
            hold((NX, NZ, CB, HALF), BF),
            hold((NX, GROUP, D), BF),
            hold((NX, D, GROUP), BF),
            hold((NX, GROUP, HALF), F32),
            hold((2, GROUP, SIDE), BF),
            hold((NX, GROUP, D), F32),
            hold((NX, GROUP, HALF), F32),
            hold((2, D, SIDE), F32),
            hold((2, PART, D), BF),
            hold((2, PART, D), BF),
            hold((NY - 1, RB, D), BF),
            hold((NY - 1, RB, D), BF),
            hold((3, RB, D), F32),
            hold((NX - 1, GROUP, D), BF),
            hold((NX - 1, GROUP, D), BF),
            hold((NZ, CB, HALF), BF),
            hold((NZ - 1, CB, HALF), BF),
            hold((2, 8, HALF), F32),
            hold((NX - 1, 8, HALF), F32),
            hold((NZ - 1, 8, HALF), F32),
            pltpu.SemaphoreType.DMA((7,)),
        ]
        + sems(NY) + sems(NZ - 1) + sems(6) + sems(NY + 2) + sems(NX + NZ - 2)
        + sems(NY) + sems(NX - 1) + sems(NZ - 1),
        compiler_params=pltpu.CompilerParams(
            collective_id=0, has_side_effects=True, vmem_limit_bytes=32 * 2**20
        ),
        name="alignment",
    )(
        regions, words, box_counts, token_counts, span_begin, span_length,
        bias_weight.reshape(1, D), logit_bias.reshape(1), loss_scale.reshape(1),
    )


def solution(mesh):
    in_specs = (
        P("dp", "text", None),
        P("dp", "text", None),
        P("dp"),
        P("dp"),
        P("dp", "text"),
        P("dp", "text"),
        P(),
        P(),
        P(),
    )
    out_specs = (P("dp", "text", None), P("dp", "text", None))
    return jax.shard_map(
        on_device, mesh=mesh, in_specs=in_specs, out_specs=out_specs, check_vma=False
    )
```

profile of v0, /device:TPU:66, one launch (start us, length us, event | category | flops | bytes accessed | tf_op | source)
XLA Modules:
  0.0 59.9 jit_solution(2943505177725393965)
XLA Ops:
  1.9 0.7 %copy.12.words = bf16[2,12,256]{2,1,0:T(8,128)(2,1)S(1)} copy(bf16[2,12,256]{2,0,1:T(2,128)(2,1)} %param.10) | data formatting | bytes 24576 | tf_op args[1]
  2.6 0.0 copy-start
  2.6 0.0 copy-start.1
  2.6 0.0 copy-start.2
  2.6 0.0 copy-start.3
  2.7 0.0 copy-start.4
  2.7 0.9 %copy.11.regions = bf16[2,75,256]{2,1,0:T(8,128)(2,1)S(1)} copy(bf16[2,75,256]{2,0,1:T(2,128)(2,1)} %param.9) | data formatting | bytes 153600 | tf_op args[0]
  3.6 0.0 copy-done
  3.6 0.0 copy-done.1
  3.6 0.0 copy-done.2
  3.6 0.0 copy-done.3
  3.7 0.0 copy-done.4
  3.7 55.0 %alignment.1 = (bf16[2,75,256]{2,1,0:T(8,128)(2,1)S(1)}, bf16[2,12,256]{2,1,0:T(8,128)(2,1)S(1)}) custom-call(bf16[2,75,256]{2,1,0:T(8,128)(2,1)S(1)} %copy.11.regions, bf16[2,12,256]{2,1,0:T(8,128)(2,1)S(1)} %copy.12.words, s32[2]{0:T(128)S(1)} %copy-done.3, s32[2]{0:T(128)S(1)} %copy-done.4, s32[2,75]{1,0:T(2,128)S(1)} %copy-done, s32[2,75]{1,0:T(2,128)S(1)} %copy-done.1, ...), custom_call_target="tpu_custom_call" | custom-call | tf_op jit(solution)/shard_map/alignment/pallas_call | solution.py:401
  58.6 0.7 %copy.13 = bf16[2,75,256]{2,0,1:T(2,128)(2,1)} copy(bf16[2,75,256]{2,1,0:T(8,128)(2,1)S(1)} %get-tuple-element.2) | data formatting | bytes 153600 | tf_op jit(solution)/shard_map/alignment/pallas_call | solution.py:401
  59.3 0.6 %copy.14 = bf16[2,12,256]{2,0,1:T(2,128)(2,1)} copy(bf16[2,12,256]{2,1,0:T(8,128)(2,1)S(1)} %get-tuple-element.3) | data formatting | bytes 24576 | tf_op jit(solution)/shard_map/alignment/pallas_call | solution.py:401
Async XLA Ops:
  2.6 1.0 %copy-start = (s32[2,75]{1,0:T(2,128)S(1)}, s32[2,75]{1,0:T(2,128)}, u32[]{:S(2)}) copy-start(s32[2,75]{1,0:T(2,128)} %begin_hbm.1) | copy-start | bytes 1804
  2.6 1.0 %copy-start.1 = (s32[2,75]{1,0:T(2,128)S(1)}, s32[2,75]{1,0:T(2,128)}, u32[]{:S(2)}) copy-start(s32[2,75]{1,0:T(2,128)} %length_hbm.1) | copy-start | bytes 1804
  2.6 1.0 %copy-start.2 = (f32[256]{0:T(256)S(1)}, f32[256]{0:T(256)}, u32[]{:S(2)}) copy-start(f32[256]{0:T(256)} %param.15) | copy-start | bytes 3076
  2.6 1.0 %copy-start.3 = (s32[2]{0:T(128)S(1)}, s32[2]{0:T(128)}, u32[]{:S(2)}) copy-start(s32[2]{0:T(128)} %box_hbm.1) | copy-start | bytes 28
  2.7 1.0 %copy-start.4 = (s32[2]{0:T(128)S(1)}, s32[2]{0:T(128)}, u32[]{:S(2)}) copy-start(s32[2]{0:T(128)} %token_hbm.1) | copy-start | bytes 28
where the time goes:
time: 60.2 us; the launch traced here: 59.9 us
  Pallas kernels  55 us (91%)
  local copies, waits for them, and re-layouts  2.98 us (5%)
  between operations  2 us (3%)
    pallas_call x1, Pallas kernels, on_device(): pl.pallas_call(kernel, out_shape=(jax.ShapeDtypeStruct((2, BOX, D), BF),...  55 us
    unnamed x12, local copies, waits for them, and re-layouts  1.67 us
    pallas_call x2, local copies, waits for them, and re-layouts, on_device(): pl.pallas_call(kernel, out_shape=(jax.ShapeDtypeStruct((2, BOX, D), BF),...  1.3 us

commit v1 on v0

--- a/solution.py
+++ b/solution.py
@@ -29,6 +29,7 @@
 Z_NEAR = Z_ORDER[:6]
 Z_FAR = Z_ORDER[6:]
 Y_SIDES = ((0, 1, 7, 2), (6, 5, 3, 4))
+GP = 384
 PART = len(Y_SIDES[0]) * RB
 
 
@@ -126,6 +127,10 @@
             value = jnp.where((row == BOX + 1) & (lane == 1), low, value)
         rows[img * BOXP : (img + 1) * BOXP, :] = value.astype(BF)
 
+    wt[...] = jnp.zeros_like(wt)
+    for side in range(2):
+        for r in range(NX):
+            g[side, r // 2, r % 2 * GP + GROUP : (r % 2 + 1) * GP, :] = jnp.zeros((GP - GROUP, SIDE), BF)
     pl.semaphore_wait(barrier, len(peers))
 
     def where(r, other):
@@ -194,11 +199,13 @@
     bias_row = bias[...]
     logit_value = logit[0]
 
+    seen, opened = set(), set()
+
     def open_group(r):
         value = toks[r].astype(F32).reshape(NZ, 2, OWN, HALF)
         value = jnp.concatenate([value[:, 0].reshape(GROUP, HALF), value[:, 1].reshape(GROUP, HALF)], axis=1)
         w[r] = value.astype(BF)
-        wt[r] = jnp.transpose(value).astype(BF)
+        wt[r // 2, :, r % 2 * GP : r % 2 * GP + GROUP] = jnp.transpose(value).astype(BF)
         column = (jnp.sum(value * bias_row, axis=1, keepdims=True) + logit_value) * LOG2E
         offset[r] = jnp.broadcast_to(column, (GROUP, HALF))
 
@@ -207,7 +214,7 @@
         rest = jnp.full((1, D - RB), missing, jnp.int32)
         return jnp.concatenate([ref[0:1, :], pad, ref[1:2, :], pad, rest], axis=1)
 
-    def score_tile(r, side):
+    def slopes(r, side):
         span = slice(side * SIDE, (side + 1) * SIDE)
         raw = jnp.dot(w[r], rows_t[:, span], preferred_element_type=F32)
         score = jnp.minimum(raw * (LOG2E / 16.0) + offset[r][:, 0:1], limit[0:1, span])
@@ -225,23 +232,20 @@
         total = slope[:, 0:HALF]
         for q in range(1, SIDE // HALF):
             total = total + slope[:, q * HALF : (q + 1) * HALF]
-        g[side] = slope.astype(BF)
-        return total
-
-    def sum_tile(r, side, total, first_of_group, first_of_side):
+        csum[r] = total if r not in seen else csum[r] + total
+        seen.add(r)
+        g[side, r // 2, r % 2 * GP : r % 2 * GP + GROUP, :] = slope.astype(BF)
+
+    def word_product(r, side):
         span = slice(side * SIDE, (side + 1) * SIDE)
-        grads = jnp.dot(g[side], rows[span, :], preferred_element_type=F32)
-        if first_of_group:
-            wp[r] = grads
-            csum[r] = total
-        else:
-            wp[r] = wp[r] + grads
-            csum[r] = csum[r] + total
-        part = jnp.dot(wt[r], g[side], preferred_element_type=F32)
-        if first_of_side:
-            rp[side] = part
-        else:
-            rp[side] = rp[side] + part
+        kept = g[side, r // 2, r % 2 * GP : r % 2 * GP + GROUP, :]
+        grads = jnp.dot(kept, rows[span, :], preferred_element_type=F32)
+        wp[r] = grads if r not in opened else wp[r] + grads
+        opened.add(r)
+
+    def region_product(pair, side, first):
+        part = jnp.dot(wt[pair], g[side, pair], preferred_element_type=F32)
+        rp[side] = part if first else rp[side] + part
 
     def close_group(r):
         column = jnp.sum(csum[r], axis=1, keepdims=True)
@@ -260,10 +264,6 @@
     }
     n_x = {k: send(tally.at[0], tally_x.at[k - 1], n_send, n_recv, k - 1, at_x(k)) for k in (1, 3, 2)}
     n_z = {k: send(tally.at[1], tally_z.at[k - 1], n_send, n_recv, 2 + k, at_z(k)) for k in Z_ORDER}
-
-    def tile(r, side):
-        total = score_tile(r, side)
-        sum_tile(r, side, total, (r, side) in ((0, 0), (1, 0), (2, 0), (3, 1)), (r, side) in ((0, 0), (2, 1)))
 
     def words_of(r):
         x_near[NX - r].wait_recv()
@@ -305,36 +305,49 @@
 
     open_group(0)
     counts = open_side(0)
-    tile(0, 0)
+    slopes(0, 0)
+    word_product(0, 0)
     pass_on(5)
     pass_on(3)
-    words_of(1)
-    tile(1, 0)
     y_copies[8].wait_recv()
     pass_on(4)
+    words_of(1)
+    slopes(1, 0)
+    word_product(1, 0)
+    region_product(0, 0, True)
     words_of(2)
-    tile(2, 0)
+    words_of(3)
     counts = counts + open_side(1)
     tally[0] = jnp.broadcast_to(counts, (8, HALF))
     for copy in n_x.values():
         copy.start()
-    tile(2, 1)
+
+    slopes(2, 0)
+    word_product(2, 0)
+    slopes(2, 1)
+    word_product(2, 1)
     send_words(2)
-    tile(0, 1)
-    words_of(3)
-    tile(1, 1)
+    slopes(3, 1)
+    word_product(3, 1)
+    region_product(1, 1, True)
+    slopes(0, 1)
+    word_product(0, 1)
+    slopes(1, 1)
+    region_product(0, 1, False)
+    other_core(1)
+    word_product(1, 1)
     send_words(1)
     for copy in n_x.values():
         copy.wait_recv()
     tally[1] = tally[0] + tally_x[0] + tally_x[1] + tally_x[2]
     for copy in n_z.values():
         copy.start()
-    tile(3, 1)
-    other_core(1)
-    tile(3, 0)
-    other_core(0)
+    slopes(3, 0)
+    word_product(3, 0)
     send_words(3)
     to_owners(1)
+    region_product(1, 0, False)
+    other_core(0)
     to_owners(0)
 
     sums = close_group(0)
@@ -420,9 +433,9 @@
             hold((8, ROWS), F32),
             hold((NX, NZ, CB, HALF), BF),
             hold((NX, GROUP, D), BF),
-            hold((NX, D, GROUP), BF),
+            hold((2, D, 2 * GP), BF),
             hold((NX, GROUP, HALF), F32),
-            hold((2, GROUP, SIDE), BF),
+            hold((2, 2, 2 * GP, SIDE), BF),
             hold((NX, GROUP, D), F32),
             hold((NX, GROUP, HALF), F32),
             hold((2, D, SIDE), F32),

time: 60.2 us -> 59.2 us (0.983)
  the two profiles are of different devices: /device:TPU:66 before, /device:TPU:2 now
where the time goes in v1:
time: 59.2 us; the launch traced here: 59 us
  Pallas kernels  54 us (91%)
  local copies, waits for them, and re-layouts  2.98 us (5%)
  between operations  2 us (3%)
    pallas_call x1, Pallas kernels, on_device(): pl.pallas_call(kernel, out_shape=(jax.ShapeDtypeStruct((2, BOX, D), BF),...  54 us
    unnamed x12, local copies, waits for them, and re-layouts  1.67 us
    pallas_call x2, local copies, waits for them, and re-layouts, on_device(): pl.pallas_call(kernel, out_shape=(jax.ShapeDtypeStruct((2, BOX, D), BF),...  1.3 us

profile of v1, /device:TPU:2, one launch (start us, length us, event | category | flops | bytes accessed | tf_op | source)
XLA Modules:
  0.0 59.0 jit_solution(2683936342015657396)
XLA Ops:
  1.9 0.7 %copy.12.words = bf16[2,12,256]{2,1,0:T(8,128)(2,1)S(1)} copy(bf16[2,12,256]{2,0,1:T(2,128)(2,1)} %param.10) | data formatting | bytes 24576 | tf_op args[1]
  2.6 0.0 copy-start
  2.6 0.0 copy-start.1
  2.6 0.0 copy-start.2
  2.6 0.0 copy-start.3
  2.7 0.0 copy-start.4
  2.7 0.9 %copy.11.regions = bf16[2,75,256]{2,1,0:T(8,128)(2,1)S(1)} copy(bf16[2,75,256]{2,0,1:T(2,128)(2,1)} %param.9) | data formatting | bytes 153600 | tf_op args[0]
  3.6 0.0 copy-done
  3.6 0.0 copy-done.1
  3.6 0.0 copy-done.2
  3.6 0.0 copy-done.3
  3.7 0.0 copy-done.4
  3.7 54.0 %alignment.1 = (bf16[2,75,256]{2,1,0:T(8,128)(2,1)S(1)}, bf16[2,12,256]{2,1,0:T(8,128)(2,1)S(1)}) custom-call(bf16[2,75,256]{2,1,0:T(8,128)(2,1)S(1)} %copy.11.regions, bf16[2,12,256]{2,1,0:T(8,128)(2,1)S(1)} %copy.12.words, s32[2]{0:T(128)S(1)} %copy-done.3, s32[2]{0:T(128)S(1)} %copy-done.4, s32[2,75]{1,0:T(2,128)S(1)} %copy-done, s32[2,75]{1,0:T(2,128)S(1)} %copy-done.1, ...), custom_call_target="tpu_custom_call" | custom-call | tf_op jit(solution)/shard_map/alignment/pallas_call | solution.py:414
  57.7 0.7 %copy.13 = bf16[2,75,256]{2,0,1:T(2,128)(2,1)} copy(bf16[2,75,256]{2,1,0:T(8,128)(2,1)S(1)} %get-tuple-element.2) | data formatting | bytes 153600 | tf_op jit(solution)/shard_map/alignment/pallas_call | solution.py:414
  58.4 0.6 %copy.14 = bf16[2,12,256]{2,0,1:T(2,128)(2,1)} copy(bf16[2,12,256]{2,1,0:T(8,128)(2,1)S(1)} %get-tuple-element.3) | data formatting | bytes 24576 | tf_op jit(solution)/shard_map/alignment/pallas_call | solution.py:414
Async XLA Ops:
  2.6 1.0 %copy-start = (s32[2,75]{1,0:T(2,128)S(1)}, s32[2,75]{1,0:T(2,128)}, u32[]{:S(2)}) copy-start(s32[2,75]{1,0:T(2,128)} %begin_hbm.1) | copy-start | bytes 1804
  2.6 1.0 %copy-start.1 = (s32[2,75]{1,0:T(2,128)S(1)}, s32[2,75]{1,0:T(2,128)}, u32[]{:S(2)}) copy-start(s32[2,75]{1,0:T(2,128)} %length_hbm.1) | copy-start | bytes 1804
  2.6 1.0 %copy-start.2 = (f32[256]{0:T(256)S(1)}, f32[256]{0:T(256)}, u32[]{:S(2)}) copy-start(f32[256]{0:T(256)} %param.15) | copy-start | bytes 3076
  2.6 1.0 %copy-start.3 = (s32[2]{0:T(128)S(1)}, s32[2]{0:T(128)}, u32[]{:S(2)}) copy-start(s32[2]{0:T(128)} %box_hbm.1) | copy-start | bytes 28
  2.7 1.0 %copy-start.4 = (s32[2]{0:T(128)S(1)}, s32[2]{0:T(128)}, u32[]{:S(2)}) copy-start(s32[2]{0:T(128)} %token_hbm.1) | copy-start | bytes 28

commit v2 on v1

--- a/solution.py
+++ b/solution.py
@@ -316,14 +316,14 @@
     word_product(1, 0)
     region_product(0, 0, True)
     words_of(2)
+
+    slopes(2, 0)
+    word_product(2, 0)
     words_of(3)
     counts = counts + open_side(1)
     tally[0] = jnp.broadcast_to(counts, (8, HALF))
     for copy in n_x.values():
         copy.start()
-
-    slopes(2, 0)
-    word_product(2, 0)
     slopes(2, 1)
     word_product(2, 1)
     send_words(2)

time: 59.2 us -> 58.8 us (level)
  no operation moved by 1% of the time
where the time goes in v2:
time: 58.8 us; the launch traced here: 58.6 us
  Pallas kernels  53.6 us (91%)
  local copies, waits for them, and re-layouts  2.98 us (5%)
  between operations  2 us (3%)
    pallas_call x1, Pallas kernels, on_device(): pl.pallas_call(kernel, out_shape=(jax.ShapeDtypeStruct((2, BOX, D), BF),...  53.6 us
    unnamed x12, local copies, waits for them, and re-layouts  1.67 us
    pallas_call x2, local copies, waits for them, and re-layouts, on_device(): pl.pallas_call(kernel, out_shape=(jax.ShapeDtypeStruct((2, BOX, D), BF),...  1.3 us

profile of v2, /device:TPU:2, one launch (start us, length us, event | category | flops | bytes accessed | tf_op | source)
XLA Modules:
  0.0 58.6 jit_solution(5634162096116415292)
XLA Ops:
  1.9 0.7 %copy.12.words = bf16[2,12,256]{2,1,0:T(8,128)(2,1)S(1)} copy(bf16[2,12,256]{2,0,1:T(2,128)(2,1)} %param.10) | data formatting | bytes 24576 | tf_op args[1]
  2.6 0.0 copy-start
  2.6 0.0 copy-start.1
  2.6 0.0 copy-start.2
  2.6 0.0 copy-start.3
  2.7 0.0 copy-start.4
  2.7 0.9 %copy.11.regions = bf16[2,75,256]{2,1,0:T(8,128)(2,1)S(1)} copy(bf16[2,75,256]{2,0,1:T(2,128)(2,1)} %param.9) | data formatting | bytes 153600 | tf_op args[0]
  3.6 0.0 copy-done
  3.6 0.0 copy-done.1
  3.6 0.0 copy-done.2
  3.6 0.0 copy-done.3
  3.7 0.0 copy-done.4
  3.7 53.6 %alignment.1 = (bf16[2,75,256]{2,1,0:T(8,128)(2,1)S(1)}, bf16[2,12,256]{2,1,0:T(8,128)(2,1)S(1)}) custom-call(bf16[2,75,256]{2,1,0:T(8,128)(2,1)S(1)} %copy.11.regions, bf16[2,12,256]{2,1,0:T(8,128)(2,1)S(1)} %copy.12.words, s32[2]{0:T(128)S(1)} %copy-done.3, s32[2]{0:T(128)S(1)} %copy-done.4, s32[2,75]{1,0:T(2,128)S(1)} %copy-done, s32[2,75]{1,0:T(2,128)S(1)} %copy-done.1, ...), custom_call_target="tpu_custom_call" | custom-call | tf_op jit(solution)/shard_map/alignment/pallas_call | solution.py:414
  57.3 0.7 %copy.13 = bf16[2,75,256]{2,0,1:T(2,128)(2,1)} copy(bf16[2,75,256]{2,1,0:T(8,128)(2,1)S(1)} %get-tuple-element.2) | data formatting | bytes 153600 | tf_op jit(solution)/shard_map/alignment/pallas_call | solution.py:414
  58.0 0.6 %copy.14 = bf16[2,12,256]{2,0,1:T(2,128)(2,1)} copy(bf16[2,12,256]{2,1,0:T(8,128)(2,1)S(1)} %get-tuple-element.3) | data formatting | bytes 24576 | tf_op jit(solution)/shard_map/alignment/pallas_call | solution.py:414
Async XLA Ops:
  2.6 1.0 %copy-start = (s32[2,75]{1,0:T(2,128)S(1)}, s32[2,75]{1,0:T(2,128)}, u32[]{:S(2)}) copy-start(s32[2,75]{1,0:T(2,128)} %begin_hbm.1) | copy-start | bytes 1804
  2.6 1.0 %copy-start.1 = (s32[2,75]{1,0:T(2,128)S(1)}, s32[2,75]{1,0:T(2,128)}, u32[]{:S(2)}) copy-start(s32[2,75]{1,0:T(2,128)} %length_hbm.1) | copy-start | bytes 1804
  2.6 1.0 %copy-start.2 = (f32[256]{0:T(256)S(1)}, f32[256]{0:T(256)}, u32[]{:S(2)}) copy-start(f32[256]{0:T(256)} %param.15) | copy-start | bytes 3076
  2.6 1.0 %copy-start.3 = (s32[2]{0:T(128)S(1)}, s32[2]{0:T(128)}, u32[]{:S(2)}) copy-start(s32[2]{0:T(128)} %box_hbm.1) | copy-start | bytes 28
  2.7 1.0 %copy-start.4 = (s32[2]{0:T(128)S(1)}, s32[2]{0:T(128)}, u32[]{:S(2)}) copy-start(s32[2]{0:T(128)} %token_hbm.1) | copy-start | bytes 28

commit v3 on v2

--- a/solution.py
+++ b/solution.py
@@ -42,8 +42,8 @@
     total = 1.0 + grown
     rest = 1.0 / total
     prob = grown * rest
-    lost = jnp.log(total) + (grown - (total - 1.0))
-    return prob * prob * (0.5 * prob + rest * lost)
+    lost = jnp.log(total) + (1.5 * grown - (total - 1.0))
+    return prob * prob * rest * lost
 
 
 def positive_slope(score):

time: 58.8 us -> 58.4 us (level)
  no operation moved by 1% of the time
where the time goes in v3:
time: 58.4 us; the launch traced here: 58.2 us
  Pallas kernels  53.2 us (91%)
  local copies, waits for them, and re-layouts  2.98 us (5%)
  between operations  2 us (3%)
    pallas_call x1, Pallas kernels, on_device(): pl.pallas_call(kernel, out_shape=(jax.ShapeDtypeStruct((2, BOX, D), BF),...  53.2 us
    unnamed x12, local copies, waits for them, and re-layouts  1.67 us
    pallas_call x2, local copies, waits for them, and re-layouts, on_device(): pl.pallas_call(kernel, out_shape=(jax.ShapeDtypeStruct((2, BOX, D), BF),...  1.3 us

profile of v3, /device:TPU:2, one launch (start us, length us, event | category | flops | bytes accessed | tf_op | source)
XLA Modules:
  0.0 58.2 jit_solution(5147215246920743197)
XLA Ops:
  1.9 0.7 %copy.12.words = bf16[2,12,256]{2,1,0:T(8,128)(2,1)S(1)} copy(bf16[2,12,256]{2,0,1:T(2,128)(2,1)} %param.10) | data formatting | bytes 24576 | tf_op args[1]
  2.6 0.0 copy-start
  2.6 0.0 copy-start.1
  2.6 0.0 copy-start.2
  2.6 0.0 copy-start.3
  2.7 0.0 copy-start.4
  2.7 0.9 %copy.11.regions = bf16[2,75,256]{2,1,0:T(8,128)(2,1)S(1)} copy(bf16[2,75,256]{2,0,1:T(2,128)(2,1)} %param.9) | data formatting | bytes 153600 | tf_op args[0]
  3.6 0.0 copy-done
  3.6 0.0 copy-done.1
  3.6 0.0 copy-done.2
  3.6 0.0 copy-done.3
  3.7 0.0 copy-done.4
  3.7 53.2 %alignment.1 = (bf16[2,75,256]{2,1,0:T(8,128)(2,1)S(1)}, bf16[2,12,256]{2,1,0:T(8,128)(2,1)S(1)}) custom-call(bf16[2,75,256]{2,1,0:T(8,128)(2,1)S(1)} %copy.11.regions, bf16[2,12,256]{2,1,0:T(8,128)(2,1)S(1)} %copy.12.words, s32[2]{0:T(128)S(1)} %copy-done.3, s32[2]{0:T(128)S(1)} %copy-done.4, s32[2,75]{1,0:T(2,128)S(1)} %copy-done, s32[2,75]{1,0:T(2,128)S(1)} %copy-done.1, ...), custom_call_target="tpu_custom_call" | custom-call | tf_op jit(solution)/shard_map/alignment/pallas_call | solution.py:414
  56.9 0.7 %copy.13 = bf16[2,75,256]{2,0,1:T(2,128)(2,1)} copy(bf16[2,75,256]{2,1,0:T(8,128)(2,1)S(1)} %get-tuple-element.2) | data formatting | bytes 153600 | tf_op jit(solution)/shard_map/alignment/pallas_call | solution.py:414
  57.6 0.6 %copy.14 = bf16[2,12,256]{2,0,1:T(2,128)(2,1)} copy(bf16[2,12,256]{2,1,0:T(8,128)(2,1)S(1)} %get-tuple-element.3) | data formatting | bytes 24576 | tf_op jit(solution)/shard_map/alignment/pallas_call | solution.py:414
Async XLA Ops:
  2.6 1.0 %copy-start = (s32[2,75]{1,0:T(2,128)S(1)}, s32[2,75]{1,0:T(2,128)}, u32[]{:S(2)}) copy-start(s32[2,75]{1,0:T(2,128)} %begin_hbm.1) | copy-start | bytes 1804
  2.6 1.0 %copy-start.1 = (s32[2,75]{1,0:T(2,128)S(1)}, s32[2,75]{1,0:T(2,128)}, u32[]{:S(2)}) copy-start(s32[2,75]{1,0:T(2,128)} %length_hbm.1) | copy-start | bytes 1804
  2.6 1.0 %copy-start.2 = (f32[256]{0:T(256)S(1)}, f32[256]{0:T(256)}, u32[]{:S(2)}) copy-start(f32[256]{0:T(256)} %param.15) | copy-start | bytes 3076
  2.6 1.0 %copy-start.3 = (s32[2]{0:T(128)S(1)}, s32[2]{0:T(128)}, u32[]{:S(2)}) copy-start(s32[2]{0:T(128)} %box_hbm.1) | copy-start | bytes 28
  2.7 1.0 %copy-start.4 = (s32[2]{0:T(128)S(1)}, s32[2]{0:T(128)}, u32[]{:S(2)}) copy-start(s32[2]{0:T(128)} %token_hbm.1) | copy-start | bytes 28
